TPU v7x, 32 devices: a whole 2x2x4 slice. The times are simulated.
32 devices in a mesh: dp: 2 (over x), pipe: 2 (over core), ctx: 8 (over z, y).
Axes of the slice: x: 2, y: 2, z: 4, core: 2. Of those that a mesh axis runs over, the one named last changes fastest.
Arguments:
- section_input: bfloat16 [2, 2, 1024, 2048], P('dp', 'pipe', 'ctx'), may hold values from -6 to 6
- section_positions: int32 [2, 2, 1024], P('dp', 'pipe', 'ctx'), may hold values from 0 to 1023, as said below
- saved_input: bfloat16 [2, 2, 1024, 2048], P('dp', 'pipe', 'ctx'), may hold values from -6 to 6
- saved_positions: int32 [2, 2, 1024], P('dp', 'pipe', 'ctx'), may hold values from 0 to 1023, as said below
- cotangent: bfloat16 [2, 2, 1024, 2048], P('dp', 'pipe', 'ctx'), may hold values from -6 to 6
- norm_gains: float32 [2, 2, 2, 2048], P(None, 'pipe'), may hold values from -2 to 2
- output_gains: float32 [2, 2, 2048], P(None, 'pipe'), may hold values from 0.25 to 2
- plan: int32 [2, 2, 2], P('dp', 'pipe'), may hold values from 0 to 1
Outputs:
- next_input: bfloat16 [2, 2, 1024, 2048], P('dp', 'pipe', 'ctx')
- upstream_grad: bfloat16 [2, 2, 1024, 2048], P('dp', 'pipe', 'ctx')
- gain_grads: float32 [2, 3, 2048], P('pipe')
Inputs may be any that keep to these rules, and one draw needn't show every extreme that they name: `section_positions`: in every sequence the first position is 0 and each later one is either one more than the position before it or 0 (a new document). `saved_positions`: in every sequence the first position is 0 and each later one is either one more than the position before it or 0 (a new document).
All inputs are finite; a program needn't handle non-finite values.
Results may differ from a plain program's by a relative error of at most 0.0075.
Values may be sent and summed in bfloat16 or wider, within the bound.
A program may use at most 64 MiB of HBM per device.

v0:
```python
import jax
import jax.numpy as jnp
from jax import lax
from jax.sharding import PartitionSpec as P

HEADS = 16
HEAD_DIM = 128
FEATURES = 2048
WINDOW = 512
TOK_DEV = 128
EPSILON = 1e-06


def passed_along(value, axis, steps):
    count = lax.axis_size(axis)
    first, last = (max(0, -steps), min(count, count - steps))
    return lax.ppermute(value, axis, [(source, source + steps) for source in range(first, last)])


def shifted(value, axis, steps):
    count = lax.axis_size(axis)
    pairs = [(source, (source + steps) % count) for source in range(count)]
    return lax.ppermute(value, axis, pairs)


def as_bfloat(values):
    narrow = lax.optimization_barrier(values.astype(jnp.bfloat16)).astype(jnp.float32)
    return values + lax.stop_gradient(narrow - values)


def attend(key_rows, key_pos, key_ok, gains, query_count):
    total_rows = key_rows.shape[0]
    first_row = total_rows - query_count
    shaped = key_rows.reshape(total_rows, HEADS, HEAD_DIM)
    normed = shaped * lax.rsqrt(jnp.mean(shaped * shaped, axis=-1, keepdims=True) + EPSILON)
    query_gain = gains[0].reshape(HEADS, HEAD_DIM)
    key_gain = gains[1].reshape(HEADS, HEAD_DIM)
    queries = as_bfloat(normed[first_row:] * query_gain)
    key_vecs = as_bfloat(normed * key_gain)
    scores = jnp.einsum("qhe,khe->hqk", queries, key_vecs) / jnp.sqrt(jnp.float32(HEAD_DIM))
    query_ids = first_row + jnp.arange(query_count, dtype=jnp.int32)
    key_ids = jnp.arange(total_rows, dtype=jnp.int32)
    distance = query_ids[:, None] - key_ids[None, :]
    query_pos = key_pos[first_row:]
    allowed = (
        (distance >= 0)
        & (distance < WINDOW)
        & (query_pos[:, None] - key_pos[None, :] == distance)
        & key_ok[None, :]
    )
    weights = jnp.where(allowed[None], jnp.exp(scores), jnp.float32(0.0))
    probability = as_bfloat(weights / jnp.sum(weights, axis=-1, keepdims=True))
    mixture = jnp.einsum("hqk,khe->qhe", probability, shaped)
    return key_rows[first_row:] + mixture.reshape(query_count, FEATURES) * gains[2]


def pick_gains(norm_gains, output_gains, lap_index):
    pair_gains = lax.dynamic_index_in_dim(norm_gains, lap_index, 0, keepdims=False)[0]
    out_gain = lax.dynamic_index_in_dim(output_gains, lap_index, 0, keepdims=False)[0]
    return jnp.concatenate([pair_gains, out_gain[None]], axis=0)


def local(
    section_input,
    section_positions,
    saved_input,
    saved_positions,
    cotangent,
    norm_gains,
    output_gains,
    plan,
):
    own_rows = section_input[0, 0]
    own_pos = section_positions[0, 0]
    saved_rows = saved_input[0, 0]
    saved_pos = saved_positions[0, 0]
    incoming = cotangent[0, 0]
    shard_rows = own_rows.shape[0]
    piece_len = min(WINDOW, shard_rows)
    piece_count = WINDOW // piece_len
    shard_index = lax.axis_index("ctx")
    pieces = (own_rows, own_pos, saved_rows, saved_pos)
    received = []
    for reach in range(1, piece_count + 1):
        received.append(passed_along((pieces[0], pieces[1], pieces[2], pieces[3]), "ctx", reach))
    ordered = received[::-1]
    ok_parts = [
        jnp.broadcast_to(shard_index >= reach, (piece_len,)) for reach in range(piece_count, 0, -1)
    ]
    key_ok = jnp.concatenate(ok_parts + [jnp.ones((shard_rows,), bool)])
    forward_gains = pick_gains(norm_gains, output_gains, plan[0, 0, 0])
    backward_gains = pick_gains(norm_gains, output_gains, plan[0, 0, 1])
    forward_keys = jnp.concatenate([piece[0] for piece in ordered] + [own_rows], axis=0).astype(
        jnp.float32
    )
    forward_pos = jnp.concatenate([piece[1] for piece in ordered] + [own_pos], axis=0)
    produced = attend(forward_keys, forward_pos, key_ok, forward_gains, shard_rows).astype(
        jnp.bfloat16
    )
    next_input = shifted(produced, "pipe", 1)
    saved_keys = jnp.concatenate([piece[2] for piece in ordered] + [saved_rows], axis=0).astype(
        jnp.float32
    )
    saved_key_pos = jnp.concatenate([piece[3] for piece in ordered] + [saved_pos], axis=0)

    def local_layer(rows, gains):
        return attend(rows, saved_key_pos, key_ok, gains, shard_rows)

    _, pullback = jax.vjp(local_layer, saved_keys, backward_gains)
    key_grads, gain_grads = pullback(incoming.astype(jnp.float32))
    own_grads = key_grads[WINDOW:]
    arriving = jnp.zeros((piece_len, FEATURES), jnp.float32)
    for reach in range(1, piece_count + 1):
        first = (piece_count - reach) * piece_len
        outgoing = key_grads[first : first + piece_len].astype(jnp.bfloat16)
        arriving = arriving + passed_along(outgoing, "ctx", -reach).astype(jnp.float32)
    own_grads = own_grads.at[shard_rows - piece_len :].add(arriving)
    upstream_grad = shifted(own_grads.astype(jnp.bfloat16), "pipe", -1)
    gain_total = lax.psum(gain_grads, ("dp", "ctx"))
    gain_total = gain_total / jnp.float32(TOK_DEV)
    return (next_input[None, None], upstream_grad[None, None], gain_total[None])


def solution(mesh):
    placed = (
        P("dp", "pipe", "ctx", None),
        P("dp", "pipe", "ctx"),
        P("dp", "pipe", "ctx", None),
        P("dp", "pipe", "ctx"),
        P("dp", "pipe", "ctx", None),
        P(None, "pipe", None, None),
        P(None, "pipe", None),
        P("dp", "pipe", None),
    )
    return jax.shard_map(
        local,
        mesh=mesh,
        in_specs=placed,
        out_specs=(
            P("dp", "pipe", "ctx", None),
            P("dp", "pipe", "ctx", None),
            P("pipe", None, None),
        ),
        check_vma=False,
    )
```

profile of v0, /device:TPU:0, one launch (start us, length us, event | category | flops | bytes accessed | tf_op | source)
XLA Modules:
  0.0 320.6 jit_solution(6539457708362573059)
XLA Ops:
  0.6 6.0 %collective-permute-start.13 = (bf16[128,2048]{1,0:T(8,128)(2,1)}, bf16[128,2048]{1,0:T(8,128)(2,1)S(1)}, u32[]{:S(2)}, u32[]{:S(2)}) collective-permute-start(bf16[128,2048]{1,0:T(8,128)(2,1)} %bitcast.86), channel_id=1, source_target_pairs={{0,4},{1,5},{2,6},{3,7},{8,12},{9,13},{10,14},{11,15},{16,20},{17,... | collective-permute-start | bytes 1572872 | tf_op jit(solution)/shard_map/ppermute | solution.py:17
  6.6 4.5 %collective-permute-start.14 = (bf16[128,2048]{1,0:T(8,128)(2,1)}, bf16[128,2048]{1,0:T(8,128)(2,1)S(1)}, u32[]{:S(2)}, u32[]{:S(2)}) collective-permute-start(bf16[128,2048]{1,0:T(8,128)(2,1)} %bitcast.87), channel_id=1, source_target_pairs={{0,3},{1,4},{2,5},{3,6},{4,7},{8,11},{9,12},{10,13},{11,14},{12,15... | collective-permute-start | bytes 1572872 | tf_op jit(solution)/shard_map/ppermute | solution.py:17
  11.1 1.3 collective-permute-start.15
  12.4 3.9 %collective-permute-start.16 = (bf16[128,2048]{1,0:T(8,128)(2,1)}, bf16[128,2048]{1,0:T(8,128)(2,1)}, u32[]{:S(2)}, u32[]{:S(2)}) collective-permute-start(bf16[128,2048]{1,0:T(8,128)(2,1)} %bitcast.89), channel_id=1, source_target_pairs={{0,1},{1,2},{2,3},{3,4},{4,5},{5,6},{6,7},{8,9},{9,10},{10,11},{11... | collective-permute-start | bytes 1572872 | tf_op jit(solution)/shard_map/ppermute | solution.py:17
  17.6 1.3 fusion.62
  21.5 2.0 copy.43
  23.5 1.3 copy.38
  26.1 2.1 copy.34
  32.1 8.5 %collective-permute-done.4 = s32[128]{0:T(128)S(1)} collective-permute-done((s32[128]{0:T(128)}, s32[128]{0:T(128)S(1)}, u32[]{:S(2)}, u32[]{:S(2)}) %collective-permute-start.4) | collective-permute-done | bytes 544 | tf_op jit(solution)/shard_map/ppermute | solution.py:17
  40.6 38.0 %collective-permute-start.5 = (s32[128]{0:T(128)}, s32[128]{0:T(128)S(1)}, u32[]{:S(2)}, u32[]{:S(2)}) collective-permute-start(s32[128]{0:T(128)} %bitcast.117), channel_id=1, source_target_pairs={{0,3},{1,4},{2,5},{3,6},{4,7},{8,11},{9,12},{10,13},{11,14},{12,15... | collective-permute-start | bytes 1544 | tf_op jit(solution)/shard_map/ppermute | solution.py:17
  78.6 1.4 collective-permute-done.5
  81.3 1.4 collective-permute-done.6
  82.7 6.2 %collective-permute-start.7 = (s32[128]{0:T(128)}, s32[128]{0:T(128)S(1)}, u32[]{:S(2)}, u32[]{:S(2)}) collective-permute-start(s32[128]{0:T(128)} %bitcast.119), channel_id=1, source_target_pairs={{0,1},{1,2},{2,3},{3,4},{4,5},{5,6},{6,7},{8,9},{9,10},{10,11},{11... | collective-permute-start | bytes 1544 | tf_op jit(solution)/shard_map/ppermute | solution.py:17
  89.0 1.4 collective-permute-done.7
  90.4 6.8 %collective-permute-start.9 = (s32[128]{0:T(128)}, s32[128]{0:T(128)S(1)}, u32[]{:S(2)}, u32[]{:S(2)}) collective-permute-start(s32[128]{0:T(128)} %bitcast.111), channel_id=1, source_target_pairs={{0,4},{1,5},{2,6},{3,7},{8,12},{9,13},{10,14},{11,15},{16,20},{17,... | collective-permute-start | bytes 1544 | tf_op jit(solution)/shard_map/ppermute | solution.py:17
  98.6 4.1 %collective-permute-start.10 = (s32[128]{0:T(128)}, s32[128]{0:T(128)S(1)}, u32[]{:S(2)}, u32[]{:S(2)}) collective-permute-start(s32[128]{0:T(128)} %bitcast.112), channel_id=1, source_target_pairs={{0,3},{1,4},{2,5},{3,6},{4,7},{8,11},{9,12},{10,13},{11,14},{12,15... | collective-permute-start | bytes 1544 | tf_op jit(solution)/shard_map/ppermute | solution.py:17
  102.8 1.4 collective-permute-done.10
  104.2 3.4 %collective-permute-start.11 = (s32[128]{0:T(128)}, s32[128]{0:T(128)S(1)}, u32[]{:S(2)}, u32[]{:S(2)}) collective-permute-start(s32[128]{0:T(128)} %bitcast.113), channel_id=1, source_target_pairs={{0,2},{1,3},{2,4},{3,5},{4,6},{5,7},{8,10},{9,11},{10,12},{11,13},... | collective-permute-start | bytes 1544 | tf_op jit(solution)/shard_map/ppermute | solution.py:17
  107.6 1.4 collective-permute-done.11
  109.0 4.1 %collective-permute-start.12 = (s32[128]{0:T(128)}, s32[128]{0:T(128)S(1)}, u32[]{:S(2)}, u32[]{:S(2)}) collective-permute-start(s32[128]{0:T(128)} %bitcast.114), channel_id=1, source_target_pairs={{0,1},{1,2},{2,3},{3,4},{4,5},{5,6},{6,7},{8,9},{9,10},{10,11},{11... | collective-permute-start | bytes 1544 | tf_op jit(solution)/shard_map/ppermute | solution.py:17
  113.1 1.4 collective-permute-done.12
  114.5 19.6 %collective-permute-start = (bf16[128,2048]{1,0:T(8,128)(2,1)}, bf16[128,2048]{1,0:T(8,128)(2,1)}, u32[]{:S(2)}, u32[]{:S(2)}) collective-permute-start(bf16[128,2048]{1,0:T(8,128)(2,1)} %bitcast), channel_id=1, source_target_pairs={{0,4},{1,5},{2,6},{3,7},{8,12},{9,13},{10,14},{11,15},{16,20},{17,... | collective-permute-start | bytes 1572872 | tf_op jit(solution)/shard_map/ppermute | solution.py:17
  135.8 2.1 collective-permute-start.1
  138.9 2.1 collective-permute-start.2
  142.0 3.3 %collective-permute-start.3 = (bf16[128,2048]{1,0:T(8,128)(2,1)}, bf16[128,2048]{1,0:T(8,128)(2,1)}, u32[]{:S(2)}, u32[]{:S(2)}) collective-permute-start(bf16[128,2048]{1,0:T(8,128)(2,1)} %bitcast), channel_id=1, source_target_pairs={{0,1},{1,2},{2,3},{3,4},{4,5},{5,6},{6,7},{8,9},{9,10},{10,11},{11... | collective-permute-start | bytes 1572872 | tf_op jit(solution)/shard_map/ppermute | solution.py:17
  149.9 2.0 copy.42
  156.0 2.7 fusion.14
  158.8 4.1 %fusion.59 = (bf16[16,128,640]{2,1,0:T(8,128)(2,1)}, f32[16,128]{1,0:T(8,128)S(1)}, f32[16,128,640]{2,1,0:T(8,128)S(1)}) fusion(f32[16,128]{1,0:T(8,128)S(1)} %get-tuple-element.51, f32[16,128,640]{2,1,0:T(8,128)S(1)} %get-tuple-element.52, pred[128,640]{1,0:T(8,128)(4,1)S(1)} %get-tuple-element.45, f32[16,128]{1,0:T(8,128)S(1)} %multiply_divide_fusion, ...), kind=kOutput, calls=%fused_computation.121 | convolution fusion | flops 345241600 | bytes 16367616 | tf_op jit(solution)/shard_map/transpose(jvp(hqk,khe->qhe))/dot_general | solution.py:53
  162.9 3.4 %multiply_reduce_fusion.1 = (f32[16,128]{1,0:T(8,128)S(1)}, f32[128,16,128]{0,2,1:T(8,128)S(1)}) fusion(f32[640,16,128]{0,2,1:T(8,128)S(1)} %get-tuple-element.29, f32[16,128]{1,0:T(8,128)S(1)} %bitcast.104, bf16[640,16,128]{0,2,1:T(8,128)(2,1)S(1)} %get-tuple-element.30, bf16[640,16,128]{0,2,1:T(8,128)(2,1)S(1)} %constant_dynamic-update-slice_fusion.7, ...), kind=kOutput, calls=%fused_computation.58 | convolution fusion | flops 352057344 | bytes 17989632 | tf_op jit(solution)/shard_map/transpose(jvp(qhe,khe->hqk))/dot_general | solution.py:40
  166.3 3.9 %fusion.6 = (f32[16,128]{1,0:T(8,128)S(1)}, f32[640,16]{0,1:T(8,128)S(1)}, f32[16,640,128]{1,2,0:T(8,128)S(1)}) fusion(bf16[640,16,128]{0,2,1:T(8,128)(2,1)S(1)} %constant_dynamic-update-slice_fusion.7, f32[640,16]{0,1:T(8,128)S(1)} %fusion.54, f32[128,16,128]{0,2,1:T(8,128)S(1)} %get-tuple-element.38, f32[16,128]{1,0:T(8,128)S(1)} %bitcast.100, ...), kind=kOutput, calls=%fused_computation.19 | convolution fusion | flops 354930688 | bytes 21176320 | tf_op jit(solution)/shard_map/transpose(jvp(qhe,khe->hqk))/dot_general | solution.py:40
  170.3 4.0 %fusion.27 = f32[16,128]{1,0:T(8,128)S(1)} fusion(f32[128,16,128]{2,0,1:T(8,128)S(1)} %copy-done.2, bf16[640,16,128]{0,2,1:T(8,128)(2,1)S(1)} %constant_dynamic-update-slice_fusion.7, bf16[16,128,640]{2,1,0:T(8,128)(2,1)} %get-tuple-element.27, f32[16,128,640]{2,1,0:T(8,128)S(1)} %get-tuple-element.52, f32[16,128]{1,0:T(8,128)S(1)} %get-tuple-element.51, ...), kind=kOutput, calls=%fused_computation.50 | convolution fusion | flops 343930880 | bytes 11632640 | tf_op jit(solution)/shard_map/jvp(hqk,khe->qhe)/dot_general | solution.py:53
  174.3 4.9 %add_add_fusion = f32[640,16,128]{0,2,1:T(8,128)} fusion(bf16[640,16,128]{0,2,1:T(8,128)(2,1)S(1)} %constant_dynamic-update-slice_fusion.7, f32[128,16,128]{0,2,1:T(8,128)S(1)} %get-tuple-element.38, f32[16,640,128]{1,2,0:T(8,128)S(1)} %get-tuple-element.54, f32[640,16]{0,1:T(8,128)S(1)} %multiply_multiply_fusion.1, f32[16,128]{1,0:T(8,128)S(1)} %bitcast.101, ...), kind=kOutput, calls=%fused_computation.4 | convolution fusion | flops 354418688 | bytes 22732800 | tf_op jit(solution)/shard_map/transpose(jvp(hqk,khe->qhe))/dot_general | solution.py:53
  179.2 6.0 %copy.48 = f32[640,2048]{1,0:T(8,128)} copy(f32[640,2048]{0,1:T(8,128)} %bitcast.70) | data formatting | bytes 10485760 | tf_op jit(solution)/shard_map/transpose(jvp())/reshape | solution.py:34
  185.1 6.1 %fusion.60 = (bf16[640,2048]{1,0:T(8,128)(2,1)S(1)}, f32[640,2048]{1,0:T(8,128)}) fusion(f32[640,2048]{1,0:T(8,128)} %copy.48, bf16[128,2048]{1,0:T(8,128)(2,1)S(1)} %bitcast.84), kind=kLoop, calls=%fused_computation.122 | loop fusion | flops 3932160 | bytes 13631488 | tf_op jit(solution)/shard_map/convert.8
  191.2 1.4 fusion.61
  192.6 1.4 collective-permute-start.17
  194.1 1.3 collective-permute-start.18
  195.4 2.0 copy.30
  197.4 1.5 collective-permute-start.19
  198.9 2.0 copy.31
  202.2 2.0 copy.32
  207.8 2.0 copy.33
  212.9 2.8 fusion.12
  216.8 3.3 %fusion.2 = f32[16,128,128]{2,1,0:T(8,128)} fusion(bf16[640,16,128]{0,2,1:T(8,128)(2,1)S(1)} %constant_dynamic-update-slice_fusion, bf16[16,128,640]{2,1,0:T(8,128)(2,1)S(1)} %fusion.29, f32[16,128,640]{2,1,0:T(8,128)S(1)} %get-tuple-element.50, f32[16,128]{1,0:T(8,128)S(1)} %get-tuple-element.49, pred[128,640]{1,0:T(8,128)(4,1)S(1)} %get-tuple-element.46), kind=kOutput, calls=%fused_computation.13 | convolution fusion | flops 343408640 | bytes 11624448 | tf_op jit(solution)/shard_map/hqk,khe->qhe/dot_general | solution.py:53
  220.1 1.6 copy.37
  223.0 21.3 %collective-permute-done.20 = bf16[128,2048]{1,0:T(8,128)(2,1)} collective-permute-done((bf16[128,2048]{1,0:T(8,128)(2,1)}, bf16[128,2048]{1,0:T(8,128)(2,1)}, u32[]{:S(2)}, u32[]{:S(2)}) %collective-permute-start.20) | collective-permute-done | bytes 524320 | tf_op jit(solution)/shard_map/ppermute | solution.py:17
  244.3 2.2 fusion.30
  246.6 71.7 %psum.7 = f32[3,2048]{1,0:T(4,128)S(1)} all-reduce(f32[3,2048]{1,0:T(4,128)S(1)} %pad_add_fusion), channel_id=1, replica_groups=mesh['dp'=2,'pipe'=2,'ctx'=8] {'dp','ctx'}, use_global_device_ids=true, to_apply=%region_9.10 | all-reduce | flops 6144 | bytes 49152 | tf_op jit(solution)/shard_map/psum | solution.py:119
  (86 shorter events, 32.7 us)
Async XLA Ops:
  0.6 135.2 %collective-permute-start.13 = (bf16[128,2048]{1,0:T(8,128)(2,1)}, bf16[128,2048]{1,0:T(8,128)(2,1)S(1)}, u32[]{:S(2)}, u32[]{:S(2)}) collective-permute-start(bf16[128,2048]{1,0:T(8,128)(2,1)} %bitcast.86), channel_id=1, source_target_pairs={{0,4},{1,5},{2,6},{3,7},{8,12},{9,13},{10,14},{11,15},{16,20},{17,... | collective-permute-start | bytes 1572872 | tf_op jit(solution)/shard_map/ppermute | solution.py:17
  6.6 132.3 %collective-permute-start.14 = (bf16[128,2048]{1,0:T(8,128)(2,1)}, bf16[128,2048]{1,0:T(8,128)(2,1)S(1)}, u32[]{:S(2)}, u32[]{:S(2)}) collective-permute-start(bf16[128,2048]{1,0:T(8,128)(2,1)} %bitcast.87), channel_id=1, source_target_pairs={{0,3},{1,4},{2,5},{3,6},{4,7},{8,11},{9,12},{10,13},{11,14},{12,15... | collective-permute-start | bytes 1572872 | tf_op jit(solution)/shard_map/ppermute | solution.py:17
  11.1 130.9 %collective-permute-start.15 = (bf16[128,2048]{1,0:T(8,128)(2,1)}, bf16[128,2048]{1,0:T(8,128)(2,1)S(1)}, u32[]{:S(2)}, u32[]{:S(2)}) collective-permute-start(bf16[128,2048]{1,0:T(8,128)(2,1)} %bitcast.88), channel_id=1, source_target_pairs={{0,2},{1,3},{2,4},{3,5},{4,6},{5,7},{8,10},{9,11},{10,12},{11,13},... | collective-permute-start | bytes 1572872 | tf_op jit(solution)/shard_map/ppermute | solution.py:17
  12.4 137.4 %collective-permute-start.16 = (bf16[128,2048]{1,0:T(8,128)(2,1)}, bf16[128,2048]{1,0:T(8,128)(2,1)}, u32[]{:S(2)}, u32[]{:S(2)}) collective-permute-start(bf16[128,2048]{1,0:T(8,128)(2,1)} %bitcast.89), channel_id=1, source_target_pairs={{0,1},{1,2},{2,3},{3,4},{4,5},{5,6},{6,7},{8,9},{9,10},{10,11},{11... | collective-permute-start | bytes 1572872 | tf_op jit(solution)/shard_map/ppermute | solution.py:17
  16.3 24.3 %collective-permute-start.4 = (s32[128]{0:T(128)}, s32[128]{0:T(128)S(1)}, u32[]{:S(2)}, u32[]{:S(2)}) collective-permute-start(s32[128]{0:T(128)} %bitcast.116), channel_id=1, source_target_pairs={{0,4},{1,5},{2,6},{3,7},{8,12},{9,13},{10,14},{11,15},{16,20},{17,... | collective-permute-start | bytes 1544 | tf_op jit(solution)/shard_map/ppermute | solution.py:17
  40.6 39.4 %collective-permute-start.5 = (s32[128]{0:T(128)}, s32[128]{0:T(128)S(1)}, u32[]{:S(2)}, u32[]{:S(2)}) collective-permute-start(s32[128]{0:T(128)} %bitcast.117), channel_id=1, source_target_pairs={{0,3},{1,4},{2,5},{3,6},{4,7},{8,11},{9,12},{10,13},{11,14},{12,15... | collective-permute-start | bytes 1544 | tf_op jit(solution)/shard_map/ppermute | solution.py:17
  80.0 2.7 collective-permute-start.6
  82.7 7.6 %collective-permute-start.7 = (s32[128]{0:T(128)}, s32[128]{0:T(128)S(1)}, u32[]{:S(2)}, u32[]{:S(2)}) collective-permute-start(s32[128]{0:T(128)} %bitcast.119), channel_id=1, source_target_pairs={{0,1},{1,2},{2,3},{3,4},{4,5},{5,6},{6,7},{8,9},{9,10},{10,11},{11... | collective-permute-start | bytes 1544 | tf_op jit(solution)/shard_map/ppermute | solution.py:17
  90.4 8.2 %collective-permute-start.9 = (s32[128]{0:T(128)}, s32[128]{0:T(128)S(1)}, u32[]{:S(2)}, u32[]{:S(2)}) collective-permute-start(s32[128]{0:T(128)} %bitcast.111), channel_id=1, source_target_pairs={{0,4},{1,5},{2,6},{3,7},{8,12},{9,13},{10,14},{11,15},{16,20},{17,... | collective-permute-start | bytes 1544 | tf_op jit(solution)/shard_map/ppermute | solution.py:17
  98.6 5.6 %collective-permute-start.10 = (s32[128]{0:T(128)}, s32[128]{0:T(128)S(1)}, u32[]{:S(2)}, u32[]{:S(2)}) collective-permute-start(s32[128]{0:T(128)} %bitcast.112), channel_id=1, source_target_pairs={{0,3},{1,4},{2,5},{3,6},{4,7},{8,11},{9,12},{10,13},{11,14},{12,15... | collective-permute-start | bytes 1544 | tf_op jit(solution)/shard_map/ppermute | solution.py:17
  104.2 4.8 %collective-permute-start.11 = (s32[128]{0:T(128)}, s32[128]{0:T(128)S(1)}, u32[]{:S(2)}, u32[]{:S(2)}) collective-permute-start(s32[128]{0:T(128)} %bitcast.113), channel_id=1, source_target_pairs={{0,2},{1,3},{2,4},{3,5},{4,6},{5,7},{8,10},{9,11},{10,12},{11,13},... | collective-permute-start | bytes 1544 | tf_op jit(solution)/shard_map/ppermute | solution.py:17
  109.0 5.6 %collective-permute-start.12 = (s32[128]{0:T(128)}, s32[128]{0:T(128)S(1)}, u32[]{:S(2)}, u32[]{:S(2)}) collective-permute-start(s32[128]{0:T(128)} %bitcast.114), channel_id=1, source_target_pairs={{0,1},{1,2},{2,3},{3,4},{4,5},{5,6},{6,7},{8,9},{9,10},{10,11},{11... | collective-permute-start | bytes 1544 | tf_op jit(solution)/shard_map/ppermute | solution.py:17
  114.5 79.5 %collective-permute-start = (bf16[128,2048]{1,0:T(8,128)(2,1)}, bf16[128,2048]{1,0:T(8,128)(2,1)}, u32[]{:S(2)}, u32[]{:S(2)}) collective-permute-start(bf16[128,2048]{1,0:T(8,128)(2,1)} %bitcast), channel_id=1, source_target_pairs={{0,4},{1,5},{2,6},{3,7},{8,12},{9,13},{10,14},{11,15},{16,20},{17,... | collective-permute-start | bytes 1572872 | tf_op jit(solution)/shard_map/ppermute | solution.py:17
  135.8 61.6 %collective-permute-start.1 = (bf16[128,2048]{1,0:T(8,128)(2,1)}, bf16[128,2048]{1,0:T(8,128)(2,1)}, u32[]{:S(2)}, u32[]{:S(2)}) collective-permute-start(bf16[128,2048]{1,0:T(8,128)(2,1)} %bitcast), channel_id=1, source_target_pairs={{0,3},{1,4},{2,5},{3,6},{4,7},{8,11},{9,12},{10,13},{11,14},{12,15... | collective-permute-start | bytes 1572872 | tf_op jit(solution)/shard_map/ppermute | solution.py:17
  138.9 62.1 %collective-permute-start.2 = (bf16[128,2048]{1,0:T(8,128)(2,1)}, bf16[128,2048]{1,0:T(8,128)(2,1)}, u32[]{:S(2)}, u32[]{:S(2)}) collective-permute-start(bf16[128,2048]{1,0:T(8,128)(2,1)} %bitcast), channel_id=1, source_target_pairs={{0,2},{1,3},{2,4},{3,5},{4,6},{5,7},{8,10},{9,11},{10,12},{11,13},... | collective-permute-start | bytes 1572872 | tf_op jit(solution)/shard_map/ppermute | solution.py:17
  142.0 65.8 %collective-permute-start.3 = (bf16[128,2048]{1,0:T(8,128)(2,1)}, bf16[128,2048]{1,0:T(8,128)(2,1)}, u32[]{:S(2)}, u32[]{:S(2)}) collective-permute-start(bf16[128,2048]{1,0:T(8,128)(2,1)} %bitcast), channel_id=1, source_target_pairs={{0,1},{1,2},{2,3},{3,4},{4,5},{5,6},{6,7},{8,9},{9,10},{10,11},{11... | collective-permute-start | bytes 1572872 | tf_op jit(solution)/shard_map/ppermute | solution.py:17
  166.3 3.9 %copy-start.2 = (f32[128,16,128]{2,0,1:T(8,128)S(1)}, f32[128,16,128]{2,0,1:T(8,128)}, u32[]{:S(2)}) copy-start(f32[128,16,128]{2,0,1:T(8,128)} %copy.50) | copy-start | bytes 3145732
  170.3 4.0 %copy-start.3 = (bf16[16,128,640]{2,1,0:T(8,128)(2,1)S(1)}, bf16[16,128,640]{2,1,0:T(8,128)(2,1)}, u32[]{:S(2)}) copy-start(bf16[16,128,640]{2,1,0:T(8,128)(2,1)} %get-tuple-element.27) | copy-start | bytes 7864324
  179.2 6.0 %copy-start.1 = (bf16[1,1,128,2048]{3,2,1,0:T(8,128)(2,1)S(1)}, bf16[1,1,128,2048]{3,2,1,0:T(8,128)(2,1)}, u32[]{:S(2)}) copy-start(bf16[1,1,128,2048]{3,2,1,0:T(8,128)(2,1)} %param.16) | copy-start | bytes 1572868
  192.6 18.4 %copy-start = (bf16[1,1,128,2048]{2,3,1,0:T(8,128)(2,1)S(1)}, bf16[1,1,128,2048]{2,3,1,0:T(8,128)(2,1)}, u32[]{:S(2)}) copy-start(bf16[1,1,128,2048]{2,3,1,0:T(8,128)(2,1)} %copy.34) | copy-start | bytes 1572868
  192.6 30.3 %collective-permute-start.17 = (bf16[128,2048]{1,0:T(8,128)(2,1)}, bf16[128,2048]{1,0:T(8,128)(2,1)}, u32[]{:S(2)}, u32[]{:S(2)}) collective-permute-start(bf16[128,2048]{1,0:T(8,128)(2,1)} %get-tuple-element.33), channel_id=1, source_target_pairs={{1,0},{2,1},{3,2},{4,3},{5,4},{6,5},{7,6},{9,8},{10,9},{11,10},{12... | collective-permute-start | bytes 1572872 | tf_op jit(solution)/shard_map/ppermute | solution.py:17
  194.1 28.9 %collective-permute-start.18 = (bf16[128,2048]{1,0:T(8,128)(2,1)}, bf16[128,2048]{1,0:T(8,128)(2,1)}, u32[]{:S(2)}, u32[]{:S(2)}) collective-permute-start(bf16[128,2048]{1,0:T(8,128)(2,1)} %get-tuple-element.36), channel_id=1, source_target_pairs={{2,0},{3,1},{4,2},{5,3},{6,4},{7,5},{10,8},{11,9},{12,10},{13,11},... | collective-permute-start | bytes 1572872 | tf_op jit(solution)/shard_map/ppermute | solution.py:17
  197.4 25.6 %collective-permute-start.19 = (bf16[128,2048]{1,0:T(8,128)(2,1)}, bf16[128,2048]{1,0:T(8,128)(2,1)}, u32[]{:S(2)}, u32[]{:S(2)}) collective-permute-start(bf16[128,2048]{1,0:T(8,128)(2,1)} %get-tuple-element.35), channel_id=1, source_target_pairs={{3,0},{4,1},{5,2},{6,3},{7,4},{11,8},{12,9},{13,10},{14,11},{15,12... | collective-permute-start | bytes 1572872 | tf_op jit(solution)/shard_map/ppermute | solution.py:17
  201.0 43.3 %collective-permute-start.20 = (bf16[128,2048]{1,0:T(8,128)(2,1)}, bf16[128,2048]{1,0:T(8,128)(2,1)}, u32[]{:S(2)}, u32[]{:S(2)}) collective-permute-start(bf16[128,2048]{1,0:T(8,128)(2,1)} %get-tuple-element.34), channel_id=1, source_target_pairs={{4,0},{5,1},{6,2},{7,3},{12,8},{13,9},{14,10},{15,11},{20,16},{21,... | collective-permute-start | bytes 1572872 | tf_op jit(solution)/shard_map/ppermute | solution.py:17
  222.9 96.1 %collective-permute-start.8 = (bf16[128,2048]{1,0:T(8,128)(2,1)S(1)}, bf16[128,2048]{1,0:T(8,128)(2,1)S(1)}, u32[]{:S(2)}, u32[]{:S(2)}) collective-permute-start(bf16[128,2048]{1,0:T(8,128)(2,1)S(1)} %add_convert_fusion), channel_id=1, source_target_pairs={{0,8},{8,0},{1,9},{9,1},{2,10},{10,2},{3,11},{11,3},{4,12},{12,4},... | collective-permute-start | bytes 1572872 | tf_op jit(solution)/shard_map/ppermute | solution.py:23
  246.5 72.5 %collective-permute-start.21 = (bf16[128,2048]{1,0:T(8,128)(2,1)S(1)}, bf16[128,2048]{1,0:T(8,128)(2,1)S(1)}, u32[]{:S(2)}, u32[]{:S(2)}) collective-permute-start(bf16[128,2048]{1,0:T(8,128)(2,1)S(1)} %fusion.30), channel_id=1, source_target_pairs={{0,8},{8,0},{1,9},{9,1},{2,10},{10,2},{3,11},{11,3},{4,12},{12,4},... | collective-permute-start | bytes 1572872 | tf_op jit(solution)/shard_map/ppermute | solution.py:23
where the time goes:
time: 322 us; the launch traced here: 321 us
  starting transfers between devices  114 us (35%)
  blocking collectives  71.7 us (22%)
  local copies, waits for them, and re-layouts  47 us (15%)
  waiting for transfers between devices  39 us (12%)
  matrix products  29.1 us (9%)
  other arithmetic  15.1 us (5%)
  between operations  5.06 us (2%)
    ppermute x20, starting transfers between devices, passed_along(): lax.ppermute(value, axis, [(source, source + steps) for source in range(f...  113 us
    psum x1, blocking collectives, local(): gain_total = lax.psum(gain_grads, ('dp', 'ctx'))  71.7 us
    ppermute x20, waiting for transfers between devices, passed_along(): lax.ppermute(value, axis, [(source, source + steps) for source in range(f...  39 us
    unnamed x33, local copies, waits for them, and re-layouts  17.3 us
    dot_general x4, matrix products, attend(): mixture = jnp.einsum('hqk,khe->qhe', probability, shaped)  16.3 us
    ppermute x8, local copies, waits for them, and re-layouts, passed_along(): lax.ppermute(value, axis, [(source, source + steps) for source in range(f...  13.2 us
    dot_general x4, matrix products, attend(): jnp.einsum('qhe,khe->hqk', queries, key_vecs)  12.8 us
  transfers between devices with their start and end apart: 22, of which 9 were waited for; matrix products, arithmetic and copies ran while one was open for 28% of the time, Pallas kernels for 0%

commit v1 on v0

--- a/solution.py
+++ b/solution.py
@@ -116,7 +116,7 @@
         arriving = arriving + passed_along(outgoing, "ctx", -reach).astype(jnp.float32)
     own_grads = own_grads.at[shard_rows - piece_len :].add(arriving)
     upstream_grad = shifted(own_grads.astype(jnp.bfloat16), "pipe", -1)
-    gain_total = lax.psum(gain_grads, ("dp", "ctx"))
+    gain_total = jnp.sum(lax.all_gather(gain_grads, ("dp", "ctx")), axis=0)
     gain_total = gain_total / jnp.float32(TOK_DEV)
     return (next_input[None, None], upstream_grad[None, None], gain_total[None])
 

time: 322 us -> 289 us (0.90)
  blocking collectives: 71.7 us -> 38.4 us
    psum x1 -> x0, blocking collectives: 71.7 us -> none  [local(): gain_total = lax.psum(gain_grads, ('dp', 'ctx'))]
    all_gather x0 -> x1, blocking collectives: none -> 38.4 us  [local(): gain_total = jnp.sum(lax.all_gather(gain_grads, ('dp', 'ctx')), axis=0)]
  transfers between devices with their start and end apart: 22 -> 22, of which waited for: 9 -> 9; matrix products, arithmetic and copies ran while one was open for 28% -> 31% of each run, Pallas kernels for 0% -> 0%
where the time goes in v1:
time: 289 us; the launch traced here: 287 us
  starting transfers between devices  114 us (39%)
  local copies, waits for them, and re-layouts  47 us (16%)
  waiting for transfers between devices  38.9 us (13%)
  blocking collectives  38.4 us (13%)
  matrix products  29.1 us (10%)
  other arithmetic  15.2 us (5%)
  between operations  5.06 us (2%)
    ppermute x20, starting transfers between devices, passed_along(): lax.ppermute(value, axis, [(source, source + steps) for source in range(f...  113 us
    ppermute x20, waiting for transfers between devices, passed_along(): lax.ppermute(value, axis, [(source, source + steps) for source in range(f...  38.9 us
    all_gather x1, blocking collectives, local(): gain_total = jnp.sum(lax.all_gather(gain_grads, ('dp', 'ctx')), axis=0)  38.4 us
    unnamed x33, local copies, waits for them, and re-layouts  17.3 us
    dot_general x4, matrix products, attend(): mixture = jnp.einsum('hqk,khe->qhe', probability, shaped)  16.3 us
    ppermute x8, local copies, waits for them, and re-layouts, passed_along(): lax.ppermute(value, axis, [(source, source + steps) for source in range(f...  13.2 us
    dot_general x4, matrix products, attend(): jnp.einsum('qhe,khe->hqk', queries, key_vecs)  12.8 us
    another operation x1, other arithmetic  6.1 us
  transfers between devices with their start and end apart: 22, of which 9 were waited for; matrix products, arithmetic and copies ran while one was open for 31% of the time, Pallas kernels for 0%

profile of v1, /device:TPU:0, one launch (start us, length us, event | category | flops | bytes accessed | tf_op | source)
XLA Modules:
  0.0 287.3 jit_solution(7904127700236186597)
XLA Ops:
  0.6 6.0 %collective-permute-start.13 = (bf16[128,2048]{1,0:T(8,128)(2,1)}, bf16[128,2048]{1,0:T(8,128)(2,1)S(1)}, u32[]{:S(2)}, u32[]{:S(2)}) collective-permute-start(bf16[128,2048]{1,0:T(8,128)(2,1)} %bitcast.88), channel_id=1, source_target_pairs={{0,4},{1,5},{2,6},{3,7},{8,12},{9,13},{10,14},{11,15},{16,20},{17,... | collective-permute-start | bytes 1572872 | tf_op jit(solution)/shard_map/ppermute | solution.py:17
  6.6 4.5 %collective-permute-start.14 = (bf16[128,2048]{1,0:T(8,128)(2,1)}, bf16[128,2048]{1,0:T(8,128)(2,1)S(1)}, u32[]{:S(2)}, u32[]{:S(2)}) collective-permute-start(bf16[128,2048]{1,0:T(8,128)(2,1)} %bitcast.89), channel_id=1, source_target_pairs={{0,3},{1,4},{2,5},{3,6},{4,7},{8,11},{9,12},{10,13},{11,14},{12,15... | collective-permute-start | bytes 1572872 | tf_op jit(solution)/shard_map/ppermute | solution.py:17
  11.1 1.3 collective-permute-start.15
  12.4 3.9 %collective-permute-start.16 = (bf16[128,2048]{1,0:T(8,128)(2,1)}, bf16[128,2048]{1,0:T(8,128)(2,1)}, u32[]{:S(2)}, u32[]{:S(2)}) collective-permute-start(bf16[128,2048]{1,0:T(8,128)(2,1)} %bitcast.91), channel_id=1, source_target_pairs={{0,1},{1,2},{2,3},{3,4},{4,5},{5,6},{6,7},{8,9},{9,10},{10,11},{11... | collective-permute-start | bytes 1572872 | tf_op jit(solution)/shard_map/ppermute | solution.py:17
  17.6 1.3 fusion.62
  21.5 2.0 copy.64
  23.5 1.3 copy.59
  26.1 2.1 copy.55
  32.1 8.5 %collective-permute-done.4 = s32[128]{0:T(128)S(1)} collective-permute-done((s32[128]{0:T(128)}, s32[128]{0:T(128)S(1)}, u32[]{:S(2)}, u32[]{:S(2)}) %collective-permute-start.4) | collective-permute-done | bytes 544 | tf_op jit(solution)/shard_map/ppermute | solution.py:17
  40.6 38.0 %collective-permute-start.5 = (s32[128]{0:T(128)}, s32[128]{0:T(128)S(1)}, u32[]{:S(2)}, u32[]{:S(2)}) collective-permute-start(s32[128]{0:T(128)} %bitcast.119), channel_id=1, source_target_pairs={{0,3},{1,4},{2,5},{3,6},{4,7},{8,11},{9,12},{10,13},{11,14},{12,15... | collective-permute-start | bytes 1544 | tf_op jit(solution)/shard_map/ppermute | solution.py:17
  78.6 1.4 collective-permute-done.5
  81.3 1.4 collective-permute-done.6
  82.7 6.2 %collective-permute-start.7 = (s32[128]{0:T(128)}, s32[128]{0:T(128)S(1)}, u32[]{:S(2)}, u32[]{:S(2)}) collective-permute-start(s32[128]{0:T(128)} %bitcast.121), channel_id=1, source_target_pairs={{0,1},{1,2},{2,3},{3,4},{4,5},{5,6},{6,7},{8,9},{9,10},{10,11},{11... | collective-permute-start | bytes 1544 | tf_op jit(solution)/shard_map/ppermute | solution.py:17
  89.0 1.4 collective-permute-done.7
  90.4 6.8 %collective-permute-start.9 = (s32[128]{0:T(128)}, s32[128]{0:T(128)S(1)}, u32[]{:S(2)}, u32[]{:S(2)}) collective-permute-start(s32[128]{0:T(128)} %bitcast.113), channel_id=1, source_target_pairs={{0,4},{1,5},{2,6},{3,7},{8,12},{9,13},{10,14},{11,15},{16,20},{17,... | collective-permute-start | bytes 1544 | tf_op jit(solution)/shard_map/ppermute | solution.py:17
  98.6 4.1 %collective-permute-start.10 = (s32[128]{0:T(128)}, s32[128]{0:T(128)S(1)}, u32[]{:S(2)}, u32[]{:S(2)}) collective-permute-start(s32[128]{0:T(128)} %bitcast.114), channel_id=1, source_target_pairs={{0,3},{1,4},{2,5},{3,6},{4,7},{8,11},{9,12},{10,13},{11,14},{12,15... | collective-permute-start | bytes 1544 | tf_op jit(solution)/shard_map/ppermute | solution.py:17
  102.8 1.4 collective-permute-done.10
  104.2 3.4 %collective-permute-start.11 = (s32[128]{0:T(128)}, s32[128]{0:T(128)S(1)}, u32[]{:S(2)}, u32[]{:S(2)}) collective-permute-start(s32[128]{0:T(128)} %bitcast.115), channel_id=1, source_target_pairs={{0,2},{1,3},{2,4},{3,5},{4,6},{5,7},{8,10},{9,11},{10,12},{11,13},... | collective-permute-start | bytes 1544 | tf_op jit(solution)/shard_map/ppermute | solution.py:17
  107.6 1.4 collective-permute-done.11
  109.0 4.1 %collective-permute-start.12 = (s32[128]{0:T(128)}, s32[128]{0:T(128)S(1)}, u32[]{:S(2)}, u32[]{:S(2)}) collective-permute-start(s32[128]{0:T(128)} %bitcast.116), channel_id=1, source_target_pairs={{0,1},{1,2},{2,3},{3,4},{4,5},{5,6},{6,7},{8,9},{9,10},{10,11},{11... | collective-permute-start | bytes 1544 | tf_op jit(solution)/shard_map/ppermute | solution.py:17
  113.1 1.4 collective-permute-done.12
  114.5 19.6 %collective-permute-start = (bf16[128,2048]{1,0:T(8,128)(2,1)}, bf16[128,2048]{1,0:T(8,128)(2,1)}, u32[]{:S(2)}, u32[]{:S(2)}) collective-permute-start(bf16[128,2048]{1,0:T(8,128)(2,1)} %bitcast), channel_id=1, source_target_pairs={{0,4},{1,5},{2,6},{3,7},{8,12},{9,13},{10,14},{11,15},{16,20},{17,... | collective-permute-start | bytes 1572872 | tf_op jit(solution)/shard_map/ppermute | solution.py:17
  135.8 2.1 collective-permute-start.1
  138.9 2.1 collective-permute-start.2
  142.0 3.3 %collective-permute-start.3 = (bf16[128,2048]{1,0:T(8,128)(2,1)}, bf16[128,2048]{1,0:T(8,128)(2,1)}, u32[]{:S(2)}, u32[]{:S(2)}) collective-permute-start(bf16[128,2048]{1,0:T(8,128)(2,1)} %bitcast), channel_id=1, source_target_pairs={{0,1},{1,2},{2,3},{3,4},{4,5},{5,6},{6,7},{8,9},{9,10},{10,11},{11... | collective-permute-start | bytes 1572872 | tf_op jit(solution)/shard_map/ppermute | solution.py:17
  149.9 2.0 copy.63
  156.0 2.7 fusion.14
  158.8 4.1 %fusion.59 = (bf16[16,128,640]{2,1,0:T(8,128)(2,1)}, f32[16,128]{1,0:T(8,128)S(1)}, f32[16,128,640]{2,1,0:T(8,128)S(1)}) fusion(f32[16,128]{1,0:T(8,128)S(1)} %get-tuple-element.51, f32[16,128,640]{2,1,0:T(8,128)S(1)} %get-tuple-element.52, pred[128,640]{1,0:T(8,128)(4,1)S(1)} %get-tuple-element.45, f32[16,128]{1,0:T(8,128)S(1)} %multiply_divide_fusion, ...), kind=kOutput, calls=%fused_computation.121 | convolution fusion | flops 345241600 | bytes 16367616 | tf_op jit(solution)/shard_map/transpose(jvp(hqk,khe->qhe))/dot_general | solution.py:53
  162.9 3.4 %multiply_reduce_fusion.1 = (f32[16,128]{1,0:T(8,128)S(1)}, f32[128,16,128]{0,2,1:T(8,128)S(1)}) fusion(f32[640,16,128]{0,2,1:T(8,128)S(1)} %get-tuple-element.29, f32[16,128]{1,0:T(8,128)S(1)} %bitcast.106, bf16[640,16,128]{0,2,1:T(8,128)(2,1)S(1)} %get-tuple-element.30, bf16[640,16,128]{0,2,1:T(8,128)(2,1)S(1)} %constant_dynamic-update-slice_fusion.7, ...), kind=kOutput, calls=%fused_computation.58 | convolution fusion | flops 352057344 | bytes 17989632 | tf_op jit(solution)/shard_map/transpose(jvp(qhe,khe->hqk))/dot_general | solution.py:40
  166.3 3.9 %fusion.6 = (f32[16,128]{1,0:T(8,128)S(1)}, f32[640,16]{0,1:T(8,128)S(1)}, f32[16,640,128]{1,2,0:T(8,128)S(1)}) fusion(bf16[640,16,128]{0,2,1:T(8,128)(2,1)S(1)} %constant_dynamic-update-slice_fusion.7, f32[640,16]{0,1:T(8,128)S(1)} %fusion.54, f32[128,16,128]{0,2,1:T(8,128)S(1)} %get-tuple-element.38, f32[16,128]{1,0:T(8,128)S(1)} %bitcast.102, ...), kind=kOutput, calls=%fused_computation.19 | convolution fusion | flops 354930688 | bytes 21176320 | tf_op jit(solution)/shard_map/transpose(jvp(qhe,khe->hqk))/dot_general | solution.py:40
  170.3 4.0 %fusion.27 = f32[16,128]{1,0:T(8,128)S(1)} fusion(f32[128,16,128]{2,0,1:T(8,128)S(1)} %copy-done.2, bf16[640,16,128]{0,2,1:T(8,128)(2,1)S(1)} %constant_dynamic-update-slice_fusion.7, bf16[16,128,640]{2,1,0:T(8,128)(2,1)} %get-tuple-element.27, f32[16,128,640]{2,1,0:T(8,128)S(1)} %get-tuple-element.52, f32[16,128]{1,0:T(8,128)S(1)} %get-tuple-element.51, ...), kind=kOutput, calls=%fused_computation.50 | convolution fusion | flops 343930880 | bytes 11632640 | tf_op jit(solution)/shard_map/jvp(hqk,khe->qhe)/dot_general | solution.py:53
  174.3 4.9 %add_add_fusion = f32[640,16,128]{0,2,1:T(8,128)} fusion(bf16[640,16,128]{0,2,1:T(8,128)(2,1)S(1)} %constant_dynamic-update-slice_fusion.7, f32[128,16,128]{0,2,1:T(8,128)S(1)} %get-tuple-element.38, f32[16,640,128]{1,2,0:T(8,128)S(1)} %get-tuple-element.54, f32[640,16]{0,1:T(8,128)S(1)} %multiply_multiply_fusion.1, f32[16,128]{1,0:T(8,128)S(1)} %bitcast.103, ...), kind=kOutput, calls=%fused_computation.4 | convolution fusion | flops 354418688 | bytes 22732800 | tf_op jit(solution)/shard_map/transpose(jvp(hqk,khe->qhe))/dot_general | solution.py:53
  179.2 6.0 %copy.69 = f32[640,2048]{1,0:T(8,128)} copy(f32[640,2048]{0,1:T(8,128)} %bitcast.72) | data formatting | bytes 10485760 | tf_op jit(solution)/shard_map/transpose(jvp())/reshape | solution.py:34
  185.1 6.1 %fusion.60 = (bf16[640,2048]{1,0:T(8,128)(2,1)S(1)}, f32[640,2048]{1,0:T(8,128)}) fusion(f32[640,2048]{1,0:T(8,128)} %copy.69, bf16[128,2048]{1,0:T(8,128)(2,1)S(1)} %bitcast.86), kind=kLoop, calls=%fused_computation.122 | loop fusion | flops 3932160 | bytes 13631488 | tf_op jit(solution)/shard_map/convert.8
  191.2 1.4 fusion.61
  192.6 1.4 collective-permute-start.17
  194.1 1.3 collective-permute-start.18
  195.4 2.0 copy.51
  197.4 1.5 collective-permute-start.19
  198.9 2.0 copy.52
  202.2 2.0 copy.53
  207.8 2.0 copy.54
  212.9 2.8 fusion.12
  216.8 3.3 %fusion.2 = f32[16,128,128]{2,1,0:T(8,128)} fusion(bf16[640,16,128]{0,2,1:T(8,128)(2,1)S(1)} %constant_dynamic-update-slice_fusion, bf16[16,128,640]{2,1,0:T(8,128)(2,1)S(1)} %fusion.29, f32[16,128,640]{2,1,0:T(8,128)S(1)} %get-tuple-element.50, f32[16,128]{1,0:T(8,128)S(1)} %get-tuple-element.49, pred[128,640]{1,0:T(8,128)(4,1)S(1)} %get-tuple-element.46), kind=kOutput, calls=%fused_computation.13 | convolution fusion | flops 343408640 | bytes 11624448 | tf_op jit(solution)/shard_map/hqk,khe->qhe/dot_general | solution.py:53
  220.1 1.6 copy.58
  223.0 21.2 %collective-permute-done.20 = bf16[128,2048]{1,0:T(8,128)(2,1)} collective-permute-done((bf16[128,2048]{1,0:T(8,128)(2,1)}, bf16[128,2048]{1,0:T(8,128)(2,1)}, u32[]{:S(2)}, u32[]{:S(2)}) %collective-permute-start.20) | collective-permute-done | bytes 524320 | tf_op jit(solution)/shard_map/ppermute | solution.py:17
  244.3 2.2 fusion.30
  246.5 38.4 %all-gather.1 = f32[16,3,2048]{2,1,0:T(4,128)S(1)} all-gather(f32[1,3,2048]{2,1,0:T(4,128)S(1)} %add_bitcast_fusion), channel_id=2, replica_groups=mesh['dp'=2,'pipe'=2,'ctx'=8] {'dp','ctx'}, dimensions={0}, use_global_device_ids=true | all-gather | bytes 417792 | tf_op jit(solution)/shard_map/all_gather | solution.py:119
  (87 shorter events, 32.8 us)
Async XLA Ops:
  0.6 135.2 %collective-permute-start.13 = (bf16[128,2048]{1,0:T(8,128)(2,1)}, bf16[128,2048]{1,0:T(8,128)(2,1)S(1)}, u32[]{:S(2)}, u32[]{:S(2)}) collective-permute-start(bf16[128,2048]{1,0:T(8,128)(2,1)} %bitcast.88), channel_id=1, source_target_pairs={{0,4},{1,5},{2,6},{3,7},{8,12},{9,13},{10,14},{11,15},{16,20},{17,... | collective-permute-start | bytes 1572872 | tf_op jit(solution)/shard_map/ppermute | solution.py:17
  6.6 132.3 %collective-permute-start.14 = (bf16[128,2048]{1,0:T(8,128)(2,1)}, bf16[128,2048]{1,0:T(8,128)(2,1)S(1)}, u32[]{:S(2)}, u32[]{:S(2)}) collective-permute-start(bf16[128,2048]{1,0:T(8,128)(2,1)} %bitcast.89), channel_id=1, source_target_pairs={{0,3},{1,4},{2,5},{3,6},{4,7},{8,11},{9,12},{10,13},{11,14},{12,15... | collective-permute-start | bytes 1572872 | tf_op jit(solution)/shard_map/ppermute | solution.py:17
  11.1 130.9 %collective-permute-start.15 = (bf16[128,2048]{1,0:T(8,128)(2,1)}, bf16[128,2048]{1,0:T(8,128)(2,1)S(1)}, u32[]{:S(2)}, u32[]{:S(2)}) collective-permute-start(bf16[128,2048]{1,0:T(8,128)(2,1)} %bitcast.90), channel_id=1, source_target_pairs={{0,2},{1,3},{2,4},{3,5},{4,6},{5,7},{8,10},{9,11},{10,12},{11,13},... | collective-permute-start | bytes 1572872 | tf_op jit(solution)/shard_map/ppermute | solution.py:17
  12.4 137.4 %collective-permute-start.16 = (bf16[128,2048]{1,0:T(8,128)(2,1)}, bf16[128,2048]{1,0:T(8,128)(2,1)}, u32[]{:S(2)}, u32[]{:S(2)}) collective-permute-start(bf16[128,2048]{1,0:T(8,128)(2,1)} %bitcast.91), channel_id=1, source_target_pairs={{0,1},{1,2},{2,3},{3,4},{4,5},{5,6},{6,7},{8,9},{9,10},{10,11},{11... | collective-permute-start | bytes 1572872 | tf_op jit(solution)/shard_map/ppermute | solution.py:17
  16.3 24.3 %collective-permute-start.4 = (s32[128]{0:T(128)}, s32[128]{0:T(128)S(1)}, u32[]{:S(2)}, u32[]{:S(2)}) collective-permute-start(s32[128]{0:T(128)} %bitcast.118), channel_id=1, source_target_pairs={{0,4},{1,5},{2,6},{3,7},{8,12},{9,13},{10,14},{11,15},{16,20},{17,... | collective-permute-start | bytes 1544 | tf_op jit(solution)/shard_map/ppermute | solution.py:17
  40.6 39.4 %collective-permute-start.5 = (s32[128]{0:T(128)}, s32[128]{0:T(128)S(1)}, u32[]{:S(2)}, u32[]{:S(2)}) collective-permute-start(s32[128]{0:T(128)} %bitcast.119), channel_id=1, source_target_pairs={{0,3},{1,4},{2,5},{3,6},{4,7},{8,11},{9,12},{10,13},{11,14},{12,15... | collective-permute-start | bytes 1544 | tf_op jit(solution)/shard_map/ppermute | solution.py:17
  80.0 2.7 collective-permute-start.6
  82.7 7.6 %collective-permute-start.7 = (s32[128]{0:T(128)}, s32[128]{0:T(128)S(1)}, u32[]{:S(2)}, u32[]{:S(2)}) collective-permute-start(s32[128]{0:T(128)} %bitcast.121), channel_id=1, source_target_pairs={{0,1},{1,2},{2,3},{3,4},{4,5},{5,6},{6,7},{8,9},{9,10},{10,11},{11... | collective-permute-start | bytes 1544 | tf_op jit(solution)/shard_map/ppermute | solution.py:17
  90.4 8.2 %collective-permute-start.9 = (s32[128]{0:T(128)}, s32[128]{0:T(128)S(1)}, u32[]{:S(2)}, u32[]{:S(2)}) collective-permute-start(s32[128]{0:T(128)} %bitcast.113), channel_id=1, source_target_pairs={{0,4},{1,5},{2,6},{3,7},{8,12},{9,13},{10,14},{11,15},{16,20},{17,... | collective-permute-start | bytes 1544 | tf_op jit(solution)/shard_map/ppermute | solution.py:17
  98.6 5.6 %collective-permute-start.10 = (s32[128]{0:T(128)}, s32[128]{0:T(128)S(1)}, u32[]{:S(2)}, u32[]{:S(2)}) collective-permute-start(s32[128]{0:T(128)} %bitcast.114), channel_id=1, source_target_pairs={{0,3},{1,4},{2,5},{3,6},{4,7},{8,11},{9,12},{10,13},{11,14},{12,15... | collective-permute-start | bytes 1544 | tf_op jit(solution)/shard_map/ppermute | solution.py:17
  104.2 4.8 %collective-permute-start.11 = (s32[128]{0:T(128)}, s32[128]{0:T(128)S(1)}, u32[]{:S(2)}, u32[]{:S(2)}) collective-permute-start(s32[128]{0:T(128)} %bitcast.115), channel_id=1, source_target_pairs={{0,2},{1,3},{2,4},{3,5},{4,6},{5,7},{8,10},{9,11},{10,12},{11,13},... | collective-permute-start | bytes 1544 | tf_op jit(solution)/shard_map/ppermute | solution.py:17
  109.0 5.6 %collective-permute-start.12 = (s32[128]{0:T(128)}, s32[128]{0:T(128)S(1)}, u32[]{:S(2)}, u32[]{:S(2)}) collective-permute-start(s32[128]{0:T(128)} %bitcast.116), channel_id=1, source_target_pairs={{0,1},{1,2},{2,3},{3,4},{4,5},{5,6},{6,7},{8,9},{9,10},{10,11},{11... | collective-permute-start | bytes 1544 | tf_op jit(solution)/shard_map/ppermute | solution.py:17
  114.5 79.5 %collective-permute-start = (bf16[128,2048]{1,0:T(8,128)(2,1)}, bf16[128,2048]{1,0:T(8,128)(2,1)}, u32[]{:S(2)}, u32[]{:S(2)}) collective-permute-start(bf16[128,2048]{1,0:T(8,128)(2,1)} %bitcast), channel_id=1, source_target_pairs={{0,4},{1,5},{2,6},{3,7},{8,12},{9,13},{10,14},{11,15},{16,20},{17,... | collective-permute-start | bytes 1572872 | tf_op jit(solution)/shard_map/ppermute | solution.py:17
  135.8 61.6 %collective-permute-start.1 = (bf16[128,2048]{1,0:T(8,128)(2,1)}, bf16[128,2048]{1,0:T(8,128)(2,1)}, u32[]{:S(2)}, u32[]{:S(2)}) collective-permute-start(bf16[128,2048]{1,0:T(8,128)(2,1)} %bitcast), channel_id=1, source_target_pairs={{0,3},{1,4},{2,5},{3,6},{4,7},{8,11},{9,12},{10,13},{11,14},{12,15... | collective-permute-start | bytes 1572872 | tf_op jit(solution)/shard_map/ppermute | solution.py:17
  138.9 62.1 %collective-permute-start.2 = (bf16[128,2048]{1,0:T(8,128)(2,1)}, bf16[128,2048]{1,0:T(8,128)(2,1)}, u32[]{:S(2)}, u32[]{:S(2)}) collective-permute-start(bf16[128,2048]{1,0:T(8,128)(2,1)} %bitcast), channel_id=1, source_target_pairs={{0,2},{1,3},{2,4},{3,5},{4,6},{5,7},{8,10},{9,11},{10,12},{11,13},... | collective-permute-start | bytes 1572872 | tf_op jit(solution)/shard_map/ppermute | solution.py:17
  142.0 65.8 %collective-permute-start.3 = (bf16[128,2048]{1,0:T(8,128)(2,1)}, bf16[128,2048]{1,0:T(8,128)(2,1)}, u32[]{:S(2)}, u32[]{:S(2)}) collective-permute-start(bf16[128,2048]{1,0:T(8,128)(2,1)} %bitcast), channel_id=1, source_target_pairs={{0,1},{1,2},{2,3},{3,4},{4,5},{5,6},{6,7},{8,9},{9,10},{10,11},{11... | collective-permute-start | bytes 1572872 | tf_op jit(solution)/shard_map/ppermute | solution.py:17
  166.3 3.9 %copy-start.2 = (f32[128,16,128]{2,0,1:T(8,128)S(1)}, f32[128,16,128]{2,0,1:T(8,128)}, u32[]{:S(2)}) copy-start(f32[128,16,128]{2,0,1:T(8,128)} %copy.71) | copy-start | bytes 3145732
  170.3 4.0 %copy-start.3 = (bf16[16,128,640]{2,1,0:T(8,128)(2,1)S(1)}, bf16[16,128,640]{2,1,0:T(8,128)(2,1)}, u32[]{:S(2)}) copy-start(bf16[16,128,640]{2,1,0:T(8,128)(2,1)} %get-tuple-element.27) | copy-start | bytes 7864324
  179.2 6.0 %copy-start.1 = (bf16[1,1,128,2048]{3,2,1,0:T(8,128)(2,1)S(1)}, bf16[1,1,128,2048]{3,2,1,0:T(8,128)(2,1)}, u32[]{:S(2)}) copy-start(bf16[1,1,128,2048]{3,2,1,0:T(8,128)(2,1)} %param.16) | copy-start | bytes 1572868
  192.6 18.4 %copy-start = (bf16[1,1,128,2048]{2,3,1,0:T(8,128)(2,1)S(1)}, bf16[1,1,128,2048]{2,3,1,0:T(8,128)(2,1)}, u32[]{:S(2)}) copy-start(bf16[1,1,128,2048]{2,3,1,0:T(8,128)(2,1)} %copy.55) | copy-start | bytes 1572868
  192.6 30.4 %collective-permute-start.17 = (bf16[128,2048]{1,0:T(8,128)(2,1)}, bf16[128,2048]{1,0:T(8,128)(2,1)}, u32[]{:S(2)}, u32[]{:S(2)}) collective-permute-start(bf16[128,2048]{1,0:T(8,128)(2,1)} %get-tuple-element.33), channel_id=1, source_target_pairs={{1,0},{2,1},{3,2},{4,3},{5,4},{6,5},{7,6},{9,8},{10,9},{11,10},{12... | collective-permute-start | bytes 1572872 | tf_op jit(solution)/shard_map/ppermute | solution.py:17
  194.1 28.9 %collective-permute-start.18 = (bf16[128,2048]{1,0:T(8,128)(2,1)}, bf16[128,2048]{1,0:T(8,128)(2,1)}, u32[]{:S(2)}, u32[]{:S(2)}) collective-permute-start(bf16[128,2048]{1,0:T(8,128)(2,1)} %get-tuple-element.36), channel_id=1, source_target_pairs={{2,0},{3,1},{4,2},{5,3},{6,4},{7,5},{10,8},{11,9},{12,10},{13,11},... | collective-permute-start | bytes 1572872 | tf_op jit(solution)/shard_map/ppermute | solution.py:17
  197.4 25.6 %collective-permute-start.19 = (bf16[128,2048]{1,0:T(8,128)(2,1)}, bf16[128,2048]{1,0:T(8,128)(2,1)}, u32[]{:S(2)}, u32[]{:S(2)}) collective-permute-start(bf16[128,2048]{1,0:T(8,128)(2,1)} %get-tuple-element.35), channel_id=1, source_target_pairs={{3,0},{4,1},{5,2},{6,3},{7,4},{11,8},{12,9},{13,10},{14,11},{15,12... | collective-permute-start | bytes 1572872 | tf_op jit(solution)/shard_map/ppermute | solution.py:17
  201.0 43.3 %collective-permute-start.20 = (bf16[128,2048]{1,0:T(8,128)(2,1)}, bf16[128,2048]{1,0:T(8,128)(2,1)}, u32[]{:S(2)}, u32[]{:S(2)}) collective-permute-start(bf16[128,2048]{1,0:T(8,128)(2,1)} %get-tuple-element.34), channel_id=1, source_target_pairs={{4,0},{5,1},{6,2},{7,3},{12,8},{13,9},{14,10},{15,11},{20,16},{21,... | collective-permute-start | bytes 1572872 | tf_op jit(solution)/shard_map/ppermute | solution.py:17
  222.9 62.8 %collective-permute-start.8 = (bf16[128,2048]{1,0:T(8,128)(2,1)S(1)}, bf16[128,2048]{1,0:T(8,128)(2,1)S(1)}, u32[]{:S(2)}, u32[]{:S(2)}) collective-permute-start(bf16[128,2048]{1,0:T(8,128)(2,1)S(1)} %add_convert_fusion), channel_id=1, source_target_pairs={{0,8},{8,0},{1,9},{9,1},{2,10},{10,2},{3,11},{11,3},{4,12},{12,4},... | collective-permute-start | bytes 1572872 | tf_op jit(solution)/shard_map/ppermute | solution.py:23
  246.5 39.2 %collective-permute-start.21 = (bf16[128,2048]{1,0:T(8,128)(2,1)S(1)}, bf16[128,2048]{1,0:T(8,128)(2,1)S(1)}, u32[]{:S(2)}, u32[]{:S(2)}) collective-permute-start(bf16[128,2048]{1,0:T(8,128)(2,1)S(1)} %fusion.30), channel_id=1, source_target_pairs={{0,8},{8,0},{1,9},{9,1},{2,10},{10,2},{3,11},{11,3},{4,12},{12,4},... | collective-permute-start | bytes 1572872 | tf_op jit(solution)/shard_map/ppermute | solution.py:23
